TPU v7x, 128 devices: a whole 4x4x4 slice. The times are simulated.
128 devices in a mesh: row: 8 (over z_hi, y), col: 4 (over z_lo, core), layer: 4 (over x).
Axes of the slice: x: 4, y: 4, z: 4 (z_hi: 2, z_lo: 2; z = z_hi * 2 + z_lo), core: 2. Of those that a mesh axis runs over, the one named last changes fastest.
Arguments:
- a_tiles: bfloat16 [8192, 12288], P('row', ('col', 'layer')), may hold values from -6 to 6
- a_occ: int32 [64, 96], P('row', ('col', 'layer')), may hold values from 0 to 1, as said below
- b_tiles: bfloat16 [4, 3072, 8192], P('layer', 'row', 'col'), may hold values from -0.09375 to 0.09375
- b_occ: int32 [4, 24, 64], P('layer', 'row', 'col'), may hold values from 0 to 1, as said below
Outputs:
- product: float32 [8192, 8192], P('row', ('col', 'layer'))
Inputs may be any that keep to these rules, and one draw needn't show every extreme that they name: `a_occ`: 1 marks a tile of A that is present; a tile marked 0 is absent and its slot in a_tiles holds values that are not part of A. The 8 x 6 tiles of one device's block of A hold at most 24 present tiles, and some device's block holds exactly 24. `b_occ`: 1 marks a tile of B that is present; a tile marked 0 is absent and its slot in b_tiles holds values that are not part of B.
All inputs are finite; a program needn't handle non-finite values.
Results may differ from a plain program's by a relative error of at most 0.0003.
Values may be sent and summed in bfloat16 or wider, within the bound.
A program may use at most 128 MiB of HBM per device.

v0:
```python
import jax
import jax.numpy as jnp
from jax import lax
from jax.sharding import PartitionSpec as P


def zero_absent(tile_data, occupancy):
    full_shape = tile_data.shape
    leading = full_shape[:-2]
    row_count = full_shape[-2]
    col_count = full_shape[-1]
    tile_rows = occupancy.shape[-2]
    tile_cols = occupancy.shape[-1]
    tiled = tile_data.reshape(
        leading + (tile_rows, row_count // tile_rows, tile_cols, col_count // tile_cols)
    )
    present = occupancy.astype(tile_data.dtype)[..., :, None, :, None]
    return (tiled * present).reshape(full_shape)


def shards(a_tiles, a_occ, b_tiles, b_occ):
    a_kept = zero_absent(a_tiles, a_occ)
    b_kept = zero_absent(b_tiles, b_occ)
    group_width = a_kept.shape[1]
    spread = lax.all_to_all(b_kept, "layer", split_axis=2, concat_axis=0, tiled=True)
    stacked = lax.all_gather(spread, "row", axis=1, tiled=True)
    layers = stacked.shape[0]
    zero_sum = jnp.zeros((a_kept.shape[0], stacked.shape[2]), jnp.float32)
    running = zero_sum
    a_piece = lax.all_gather(a_kept, ("col", "layer"), axis=1, tiled=True)
    first_group = jnp.int32(0) // group_width
    for offset in range(a_piece.shape[1] // group_width):
        group_index = first_group + offset
        layer_slab = group_index % layers
        row_start = group_index // layers * group_width
        a_block = a_piece[:, offset * group_width : (offset + 1) * group_width]
        b_block = lax.dynamic_slice(
            stacked, (layer_slab, row_start, 0), (1, group_width, stacked.shape[2])
        )[0]
        running = running + jnp.dot(a_block, b_block, preferred_element_type=jnp.float32)
    return running


def solution(mesh):
    placed = (
        P("row", ("col", "layer")),
        P("row", ("col", "layer")),
        P("layer", "row", "col"),
        P("layer", "row", "col"),
    )
    return jax.shard_map(
        shards, mesh=mesh, in_specs=placed, out_specs=P("row", ("col", "layer")), check_vma=False
    )
```

profile of v0, /device:TPU:0, one launch (start us, length us, event | category | flops | bytes accessed | tf_op | source)
XLA Modules:
  0.0 452.0 jit_solution(9755838920835022020)
XLA Ops:
  8.2 3.2 mul.48
  11.4 7.9 %copy.48 = bf16[1,384,2048]{1,0,2:T(2,128)(2,1)S(1)} copy(bf16[1,384,2048]{2,1,0:T(8,128)(2,1)} %mul.48) | data formatting | bytes 3145728 | tf_op jit(solution)/shard_map/mul | solution.py:18
  19.9 34.5 %reduce = bf16[2048,384]{1,0:T(8,128)(2,1)} reduce(bf16[2048,1,384]{2,1,0:T(2,128)(2,1)S(1)} %bitcast.81, bf16[]{:T(256)} %broadcast.23), dimensions={1}, to_apply=%bitcast.78.reduce_sub_computation | reduce | bytes 3145730
  54.4 2.4 reshape.16
  56.8 25.0 %all_to_all.18 = bf16[4,2,98304]{2,1,0:T(2,128)(2,1)} all-to-all(bf16[4,2,98304]{2,1,0:T(2,128)(2,1)S(1)} %reshape.16), channel_id=1, replica_groups=mesh['row'=8,'col'=4,'layer'=4] {'layer'}, dimensions={0} | all-to-all | bytes 3145728 | tf_op jit(solution)/shard_map/all_to_all | solution.py:25
  81.8 3.1 reshape.17
  90.2 160.2 %all-gather.6.cloned.1.call-done = bf16[4,1,3072,512]{2,3,0,1:T(8,128)(2,1)} async-done(((bf16[4,1,384,512]{2,3,0,1:T(8,128)(2,1)}), bf16[4,1,3072,512]{2,3,0,1:T(8,128)(2,1)}) %all-gather.6.cloned.1.call-update) | async-done | bytes 12582928 | tf_op jit(solution)/shard_map/all_gather | solution.py:26
  250.4 138.7 %all-gather.4.cloned.1.call-done = bf16[1024,12288]{0,1:T(8,128)(2,1)} async-done(((bf16[1024,768]{0,1:T(8,128)(2,1)}), bf16[1024,12288]{0,1:T(8,128)(2,1)}) %all-gather.4.cloned.1.call-update) | async-done | bytes 25165840 | tf_op jit(solution)/shard_map/all_gather | solution.py:30
  389.1 2.8 fusion.1
  391.9 3.3 fusion.3
  395.2 3.4 fusion.5
  399.4 2.2 fusion.7
  401.6 2.2 fusion.9
  403.7 2.2 fusion.11
  405.9 2.2 fusion.13
  408.1 2.2 fusion.15
  410.3 3.5 fusion.17
  413.7 3.5 fusion.19
  417.2 3.5 fusion.21
  420.7 3.8 fusion.23
  424.4 3.5 fusion.25
  427.9 3.5 fusion.27
  431.4 3.5 fusion.29
  434.9 10.3 %add_add_fusion = f32[1024,512]{1,0:T(8,128)} fusion(f32[1024,512]{1,0:T(8,128)S(1)} %fusion.1, f32[1024,512]{1,0:T(8,128)S(1)} %fusion.3, f32[1024,512]{1,0:T(8,128)S(1)} %fusion.5, f32[1024,512]{1,0:T(8,128)S(1)} %fusion.7, f32[1024,512]{1,0:T(8,128)S(1)} %fusion.9, f32[1024,512]{1,0:T(8,128)S(1)} %fusion.11, f32[1024,512]{1,0:T(8,128)S(1)} %fusion.13, ...), kind=kOutput, calls=%fused_computation | convolution fusion | flops 813170688 | bytes 35913728 | tf_op jit(solution)/shard_map/dot_general | solution.py:40
  (21 shorter events, 8.5 us)
Async XLA Ops:
  6.5 243.9 %all-gather.6.cloned.1.call-start = ((), (), s32[]{:S(2)}) async-start(), calls=%async_computation.2 | async-start | bytes 14155776 | tf_op jit(solution)/shard_map/all_gather | solution.py:26
  84.8 1.5 copy-start.2
  86.2 1.4 copy-start
  86.3 302.8 %all-gather.4.cloned.1.call-start = ((), (), s32[]{:S(2)}) async-start(), calls=%async_computation.1 | async-start | bytes 26738688 | tf_op jit(solution)/shard_map/all_gather | solution.py:30
  389.1 10.3 %copy-start.1 = (bf16[1024,12288]{0,1:T(8,128)(2,1)S(1)}, bf16[1024,12288]{0,1:T(8,128)(2,1)}, u32[]{:S(2)}) copy-start(bf16[1024,12288]{0,1:T(8,128)(2,1)} %all-gather.4.cloned.1.call-done) | copy-start | bytes 75497472
Sparse Core Ops, SparseCore 0:
  86.4 163.9 all-gather.5
  252.1 136.9 all-gather.3
where the time goes:
time: 454 us; the launch traced here: 452 us
  waiting for transfers between devices  299 us (66%)
  matrix products  55.2 us (12%)
  other arithmetic  39.7 us (9%)
  blocking collectives  25 us (6%)
  local copies, waits for them, and re-layouts  19.7 us (4%)
  between operations  13.5 us (3%)
    all_gather x1, waiting for transfers between devices, shards(): stacked = lax.all_gather(spread, 'row', axis=1, tiled=True)  160 us
    all_gather x1, waiting for transfers between devices, shards(): a_piece = lax.all_gather(a_kept, ('col', 'layer'), axis=1, tiled=True)  139 us
    dot_general x16, matrix products, shards(): jnp.dot(a_block, b_block, preferred_element_type=jnp.float32)  55.2 us
    unnamed x1, other arithmetic  34.5 us
    all_to_all x1, blocking collectives, shards(): lax.all_to_all(b_kept, 'layer', split_axis=2, concat_axis=0, tiled=True)  25 us
    unnamed x12, local copies, waits for them, and re-layouts  10.4 us
    mul x4, local copies, waits for them, and re-layouts, zero_absent(): return (tiled * present).reshape(full_shape)  9.2 us
  transfers between devices with their start and end apart: 2, of which 2 were waited for; matrix products, arithmetic and copies ran while one was open for 1% of the time, Pallas kernels for 0%

commit v1 on v0

v1 whole, which is shorter than its diff:
```python
import jax
import jax.numpy as jnp
from jax import lax
from jax.experimental import pallas as pl
from jax.experimental.pallas import tpu as pltpu
from jax.sharding import PartitionSpec as P

MESH = pl.DeviceIdType.MESH
TILE = 128
ROWT = 8
GROUPT = 6
CAPS = 24
HALF = CAPS // 2
SLOTS = ROWT * GROUPT
BROWT = 3
COLT = 16
PIECE = BROWT * TILE
GROUP = GROUPT * TILE
ROWS = ROWT * TILE
NX = 4
NCOLS = COLT * TILE // NX
MIB = 1024 * 1024


def pack_kernel(a_occ, b_occ, a_ref, b_ref, packed, slots, kept):
    def place(t, used):
        i, j = t // GROUPT, lax.rem(t, GROUPT)
        row = pl.multiple_of(i * TILE, TILE)
        col = pl.multiple_of(j * TILE, TILE)
        packed[used] = a_ref[pl.ds(row, TILE), pl.ds(col, TILE)]
        here = a_occ[i, j]
        slots[t] = jnp.where(here != 0, used, CAPS)
        return used + jnp.where(here != 0, 1, 0)

    lax.fori_loop(0, SLOTS, place, jnp.int32(0))
    packed[CAPS] = jnp.zeros((TILE, TILE), jnp.bfloat16)
    for t in range(SLOTS, 128):
        slots[t] = CAPS
    for i in range(BROWT):
        for j in range(COLT):
            tile = b_ref[0, i * TILE : (i + 1) * TILE, j * TILE : (j + 1) * TILE]
            part, at = divmod(j, COLT // NX)
            present = b_occ[0, i, j] != 0
            kept[part, i * TILE : (i + 1) * TILE, at * TILE : (at + 1) * TILE] = jnp.where(
                present, tile, jnp.zeros_like(tile)
            )


def pack(a_tiles, a_occ, b_tiles, b_occ):
    vmem = pl.BlockSpec(memory_space=pltpu.VMEM)
    smem = pl.BlockSpec(memory_space=pltpu.SMEM)
    return pl.pallas_call(
        pack_kernel,
        out_shape=(
            jax.ShapeDtypeStruct((CAPS + 1, TILE, TILE), jnp.bfloat16),
            jax.ShapeDtypeStruct((128,), jnp.int32),
            jax.ShapeDtypeStruct((NX, PIECE, NCOLS), jnp.bfloat16),
        ),
        in_specs=[smem, smem, vmem, vmem],
        out_specs=(vmem, smem, vmem),
        compiler_params=pltpu.CompilerParams(vmem_limit_bytes=32 * MIB),
        name="pack",
    )(a_occ, b_occ, a_tiles, b_tiles)


A_KEYS = [(dx, dz, dc) for dx in range(4) for dz in range(2) for dc in range(2)]


def product_kernel(packed, slots, kept, out, *scratch):
    a_buf = dict(zip(A_KEYS, scratch[:16]))
    m_buf = dict(zip(A_KEYS, scratch[16:32]))
    b_buf, dense, send_sem, recv_sem, local_sem = scratch[32:]
    row, col, x = lax.axis_index("row"), lax.axis_index("col"), lax.axis_index("layer")
    zh, y, zl, c = row // 4, lax.rem(row, 4), col // 2, lax.rem(col, 2)

    def at_row(dz=0, dy=0):
        return lax.rem(zh + dz, 2) * 4 + lax.rem(y + dy + 4, 4)

    def at_col(dz=0, dc=0):
        return lax.rem(zl + dz, 2) * 2 + lax.rem(c + dc, 2)

    def at_layer(dx):
        return lax.rem(x + dx + 4, 4)

    def device(dx=0, dy=0, dzh=0, dzl=0, dc=0):
        return (at_row(dzh, dy), at_col(dzl, dc), at_layer(dx))

    neighbours = [
        dict(dx=1), dict(dx=-1), dict(dx=2), dict(dy=1), dict(dy=-1), dict(dzh=1), dict(dzl=1), dict(dc=1)
    ]
    barrier = pltpu.get_barrier_semaphore()
    for n in neighbours:
        pl.semaphore_signal(barrier, inc=1, device_id=device(**n), device_id_type=MESH)

    sends = []
    numbers = {}
    copies = {}

    def number(key):
        return numbers.setdefault(key, len(numbers))

    def send(key, src, dst, **to):
        n = number(key)
        copy = pltpu.make_async_remote_copy(
            src_ref=src, dst_ref=dst, send_sem=send_sem.at[n], recv_sem=recv_sem.at[n],
            device_id=device(**to), device_id_type=MESH,
        )
        copy.start()
        copies[key] = copy
        sends.append(copy)

    def wait(*keys):
        for key in keys:
            copies[key].wait_recv()

    def piece(dl, dz, dy, half=None):
        r = at_row(dz, dy)
        if half is None:
            return b_buf.at[at_layer(dl), pl.ds(pl.multiple_of(r * PIECE, PIECE), PIECE)]
        size = PIECE // 2
        start = pl.multiple_of(r * PIECE + half * size, size)
        return b_buf.at[at_layer(dl), pl.ds(start, size)]

    def tiles(key, half):
        return a_buf[key].at[pl.ds(half * HALF, HALF)]

    local = [
        pltpu.make_async_copy(packed, a_buf[0, 0, 0], local_sem.at[0]),
        pltpu.make_async_copy(slots, m_buf[0, 0, 0], local_sem.at[1]),
        pltpu.make_async_copy(kept.at[x], piece(0, 0, 0), local_sem.at[2]),
    ]
    for copy in local:
        copy.start()
    for key in A_KEYS[1:]:
        a_buf[key][CAPS] = jnp.zeros((TILE, TILE), jnp.bfloat16)
    pl.semaphore_wait(barrier, len(neighbours))

    def b_spread(d):
        send(("b", -d % 4, 0, 0), kept.at[at_layer(d)], b_buf.at[x, pl.ds(pl.multiple_of(row * PIECE, PIECE), PIECE)], dx=d)

    def b_y(dl, dz):
        src = kept.at[x] if (dl, dz) == (0, 0) else piece(dl, dz, 0)
        for d in (1, -1):
            send(("b", dl, dz, -d % 4), src, piece(dl, dz, 0), dy=d)

    def b_z(dl, dy):
        src = kept.at[x] if (dl, dy) == (0, 0) else piece(dl, 0, dy)
        send(("b", dl, 1, dy), src, piece(dl, 0, dy), dzh=1)

    def b_on(dl):
        send(("b", dl, 0, 2, 0), piece(dl, 0, -1, 0), piece(dl, 0, -1, 0), dy=1)
        send(("b", dl, 0, 2, 1), piece(dl, 0, 1, 1), piece(dl, 0, 1, 1), dy=-1)

    def a_z():
        send(("m", 0, 1, 0), slots, m_buf[0, 1, 0], dzl=1)
        for h in range(2):
            send(("a", 0, 1, 0, h), packed.at[pl.ds(h * HALF, HALF)], tiles((0, 1, 0), h), dzl=1)

    def a_x(dz):
        for d in (1, -1):
            key = (-d % 4, dz, 0)
            send(("m",) + key, slots if dz == 0 else m_buf[0, 1, 0], m_buf[key], dx=d)
        for h in range(2):
            src = packed.at[pl.ds(h * HALF, HALF)] if dz == 0 else tiles((0, 1, 0), h)
            for d in (1, -1):
                key = (-d % 4, dz, 0)
                hh = h if d == 1 else 1 - h
                src = packed.at[pl.ds(hh * HALF, HALF)] if dz == 0 else tiles((0, 1, 0), hh)
                send(("a",) + key + (hh,), src, tiles(key, hh), dx=d)

    def a_on(dz):
        send(("m", 2, dz, 0), m_buf[3, dz, 0], m_buf[2, dz, 0], dx=1)
        send(("a", 2, dz, 0, 0), tiles((3, dz, 0), 0), tiles((2, dz, 0), 0), dx=1)
        send(("a", 2, dz, 0, 1), tiles((1, dz, 0), 1), tiles((2, dz, 0), 1), dx=-1)

    def a_core(dx, dz):
        key, other = (dx, dz, 0), (dx, dz, 1)
        own = (dx, dz) == (0, 0)
        send(("m",) + other, slots if own else m_buf[key], m_buf[other], dc=1)
        send(("a",) + other, packed.at[pl.ds(0, CAPS)] if own else a_buf[key].at[pl.ds(0, CAPS)], a_buf[other].at[pl.ds(0, CAPS)], dc=1)

    def wait_a(dx, dz):
        wait(("m", dx, dz, 0), ("a", dx, dz, 0, 0), ("a", dx, dz, 0, 1))

    def wait_a_core(dx):
        for dz in range(2):
            wait(("m", dx, dz, 1), ("a", dx, dz, 1))

    def unpack(dx):
        for dz in range(2):
            for dc in range(2):
                key = (dx, dz, dc)
                group = at_col(dz, dc)

                def tile_row(i, carry, key=key, group=group):
                    at = pl.ds(pl.multiple_of(i * TILE, TILE), TILE)
                    for j in range(GROUPT):
                        slot = m_buf[key][i * GROUPT + j]
                        dense[group, at, j * TILE : (j + 1) * TILE] = a_buf[key][slot]
                    return carry

                lax.fori_loop(0, ROWT, tile_row, 0)

    first = [True]

    def multiply(dl, dz, dp):
        group = lax.rem(zh + dz, 2) * 2 + lax.rem(y // 2 + dp, 2)
        rows = pl.ds(pl.multiple_of(group * GROUP, GROUP), GROUP)
        start = first[0]
        first[0] = False

        def columns(n, carry):
            at = pl.ds(pl.multiple_of(n * 256, 256), 256)
            term = jnp.dot(dense[group], b_buf[at_layer(dl), rows, at], preferred_element_type=jnp.float32)
            if start:
                out[:, at] = term
            else:
                out[:, at] += term
            return carry

        lax.fori_loop(0, NCOLS // 256, columns, 0)

    b_y(0, 0)
    b_z(0, 0)
    for d in (1, 3, 2):
        b_spread(d)
    a_z()
    a_core(0, 0)
    a_x(0)
    for copy in local:
        copy.wait()

    wait(("b", 0, 1, 0))
    b_y(0, 1)
    for dl in (1, 3):
        wait(("b", dl, 0, 0))
        b_z(dl, 0)
    wait(("b", 0, 0, 1), ("b", 0, 0, 3))
    b_on(0)
    b_y(1, 0)
    b_y(3, 0)
    wait_a(0, 1)
    a_x(1)
    a_core(0, 1)
    wait(("b", 2, 0, 0))
    b_z(2, 0)
    wait_a_core(0)
    unpack(0)
    multiply(0, 0, 0)
    wait(("b", 0, 1, 1), ("b", 0, 1, 3))
    multiply(0, 1, 0)
    wait(("b", 0, 0, 2, 0), ("b", 0, 0, 2, 1))
    b_z(0, 2)
    multiply(0, 0, 1)

    for dl, after in ((1, 2), (3, None), (2, None)):
        wait(("b", dl, 1, 0))
        if dl != 2:
            b_y(dl, 1)
        wait(("b", dl, 0, 1), ("b", dl, 0, 3))
        b_on(dl)
        if dl == 2:
            b_y(dl, 1)
        if after is not None:
            b_y(after, 0)
        if dl == 1:
            wait(("b", 0, 1, 2))
            multiply(0, 1, 1)
            for dz in range(2):
                wait_a(1, dz)
                wait_a(3, dz)
                a_on(dz)
                a_core(1, dz)
                a_core(3, dz)
        if dl == 2:
            for dz in range(2):
                wait_a(2, dz)
                a_core(2, dz)
        wait_a_core(dl)
        unpack(dl)
        multiply(dl, 0, 0)
        wait(("b", dl, 0, 2, 0), ("b", dl, 0, 2, 1))
        b_z(dl, 2)
        multiply(dl, 0, 1)
        wait(("b", dl, 1, 1), ("b", dl, 1, 3))
        multiply(dl, 1, 0)
        wait(("b", dl, 1, 2))
        multiply(dl, 1, 1)

    for copy in sends:
        copy.wait_send()


N_COPIES = 3 + 4 * 8 + 14 + 8 + 15


def product(packed, slots, kept):
    anywhere = pl.BlockSpec(memory_space=pl.ANY)
    return pl.pallas_call(
        product_kernel,
        out_shape=jax.ShapeDtypeStruct((ROWS, NCOLS), jnp.float32),
        in_specs=[anywhere, anywhere, anywhere],
        out_specs=pl.BlockSpec(memory_space=pltpu.VMEM),
        scratch_shapes=[pltpu.VMEM((CAPS + 1, TILE, TILE), jnp.bfloat16)] * 16
        + [pltpu.SMEM((128,), jnp.int32)] * 16
        + [
            pltpu.VMEM((NX, 8 * PIECE, NCOLS), jnp.bfloat16),
            pltpu.VMEM((4, ROWS, GROUP), jnp.bfloat16),
            pltpu.SemaphoreType.DMA((N_COPIES,)),
            pltpu.SemaphoreType.DMA((N_COPIES,)),
            pltpu.SemaphoreType.DMA((3,)),
        ],
        compiler_params=pltpu.CompilerParams(
            collective_id=0, has_side_effects=True, vmem_limit_bytes=56 * MIB
        ),
        name="product",
    )(packed, slots, kept)


def shards(a_tiles, a_occ, b_tiles, b_occ):
    return product(*pack(a_tiles, a_occ, b_tiles, b_occ))


def solution(mesh):
    placed = (
        P("row", ("col", "layer")),
        P("row", ("col", "layer")),
        P("layer", "row", "col"),
        P("layer", "row", "col"),
    )
    return jax.shard_map(
        shards, mesh=mesh, in_specs=placed, out_specs=P("row", ("col", "layer")), check_vma=False
    )
```

time: 454 us -> 148 us (0.33)
  waiting for transfers between devices: 299 us -> 0 us
  Pallas kernels: 0 us -> 138 us
  matrix products: 55.2 us -> 0 us
  other arithmetic: 39.7 us -> 0 us
  blocking collectives: 25 us -> 0 us
  between operations: 13.5 us -> 0.03 us
  local copies, waits for them, and re-layouts: 19.7 us -> 9.82 us
    all_gather x2 -> x0, waiting for transfers between devices: 299 us -> none  [the longest x1 160 us: shards(): stacked = lax.all_gather(spread, 'row', axis=1, tiled=True)]
    pallas_call x0 -> x2, Pallas kernels: none -> 138 us  [the longest x1 135 us: product(): pl.pallas_call(product_kernel, out_shape=jax.ShapeDtypeStruct((ROWS, NCOL...]
    dot_general x16 -> x0, matrix products: 55.2 us -> none  [shards(): jnp.dot(a_block, b_block, preferred_element_type=jnp.float32)]
    unnamed x1 -> x0, other arithmetic: 34.5 us -> none
    all_to_all x1 -> x0, blocking collectives: 25 us -> none  [shards(): lax.all_to_all(b_kept, 'layer', split_axis=2, concat_axis=0, tiled=True)]
    mul x4 -> x0, local copies, waits for them, and re-layouts: 9.2 us -> none  [zero_absent(): return (tiled * present).reshape(full_shape)]
    unnamed x12 -> x14, local copies, waits for them, and re-layouts: 10.4 us -> 9.82 us
  transfers between devices with their start and end apart: 2 -> 0, of which waited for: 2 -> 0; matrix products, arithmetic and copies ran while one was open for 1% -> 0% of each run, Pallas kernels for 0% -> 0%
where the time goes in v1:
time: 148 us
  Pallas kernels  138 us (93%)
  local copies, waits for them, and re-layouts  9.82 us (7%)
    pallas_call x1, Pallas kernels, product(): pl.pallas_call(product_kernel, out_shape=jax.ShapeDtypeStruct((ROWS, NCOL...  135 us
    unnamed x14, local copies, waits for them, and re-layouts  9.82 us

profile of v1, /device:TPU:0, one launch (start us, length us, event | category | flops | bytes accessed | tf_op | source)
XLA Modules:
  0.0 147.6 jit_solution(13143402562985150931)
XLA Ops:
  0.0 0.7 copy.5.b_occ
  0.7 0.0 copy-start.1
  0.7 1.4 copy-done.1
  2.1 0.0 copy-start.2
  2.1 1.4 copy-done.2
  3.5 0.0 copy-start.4
  3.5 0.7 copy-done.4
  4.2 2.7 %pack.1 = (bf16[25,128,128]{2,1,0:T(8,128)(2,1)S(1)}, s32[128]{0:T(128)S(1)}, bf16[4,384,512]{2,1,0:T(8,128)(2,1)S(1)}) custom-call(s32[8,6]{1,0:T(8,128)S(1)} %copy-done.4, s32[1,3,16]{2,1,0:T(4,128)S(1)} %copy.5.b_occ, bf16[1024,768]{1,0:T(8,128)(2,1)S(1)} %copy-done.1, bf16[1,384,2048]{2,1,0:T(8,128)(2,1)S(1)} %copy-done.2), custom_call_target="tpu_custom_call" | custom-call | tf_op jit(solution)/shard_map/pack/pallas_call | solution.py:52
  6.9 0.0 copy-start
  6.9 1.1 copy-done
  8.1 0.0 copy-start.3
  8.1 0.9 copy-done.3
  9.0 0.0 copy-start.5
  9.0 0.5 copy-done.5
  9.5 135.1 %product.1 = f32[1024,512]{1,0:T(8,128)} custom-call(bf16[25,128,128]{2,1,0:T(8,128)(2,1)} %copy-done.3, s32[128]{0:T(128)} %copy-done.5, bf16[4,384,512]{2,1,0:T(8,128)(2,1)} %copy-done), custom_call_target="tpu_custom_call" | custom-call | tf_op jit(solution)/shard_map/product/pallas_call | solution.py:299
  144.6 3.1 %copy.7 = f32[1024,512]{1,0:T(8,128)} copy(f32[1024,512]{1,0:T(8,128)} %product.1) | data formatting | bytes 4194304
Async XLA Ops:
  0.7 1.4 copy-start.1
  2.1 1.4 copy-start.2
  3.5 0.7 copy-start.4
  6.9 1.1 copy-start
  8.1 0.9 copy-start.3
  9.0 0.5 copy-start.5

commit v2 on v0

v2 whole, which is shorter than its diff:
```python
import jax
import jax.numpy as jnp
from jax import lax
from jax.experimental import pallas as pl
from jax.experimental.pallas import tpu as pltpu
from jax.sharding import PartitionSpec as P

MESH = pl.DeviceIdType.MESH
TILE = 128
ROWT = 8
GROUPT = 6
CAPS = 24
CUTS = 4
CUT = CAPS // CUTS
SLOTS = ROWT * GROUPT
BROWT = 3
COLT = 16
PIECE = BROWT * TILE
GROUP = GROUPT * TILE
ROWS = ROWT * TILE
NX = 4
NY = 4
NCOLS = COLT * TILE // NX
SIDES = 2
SIDE = NCOLS // SIDES
MIB = 1024 * 1024
OWN, OTHER = 0, 1
PARTS = 4
PART = ROWS // PARTS
LEVELS = 32767.0
SMALLEST = 1e-30

A_KEYS = [(dx, s, dc) for dx in range(4) for s in (OWN, OTHER) for dc in range(2)]
PLAN = [
    ("bs", 1, 1), ("bs", 1, 3), ("by", 1, 0), ("bs", 0, 1), ("bs", 0, 3), ("by", 0, 0), ("ax", "E", 0, 0),
    ("ax", "F", 1, 0), ("fq", 0), ("by", 1, 1), ("fq", 1), ("by", 0, 3), ("bs", 0, 2), ("by", 0, 1),
    ("ao", "F", 1, 0), ("ax", "E", 1, 0), ("fq", 2), ("ax", "E", 1, 2), ("ax", "E", 1, 1), ("bo", 0, 0),
    ("ax", "F", 1, 1), ("ax", "F", 1, 2), ("ac", 0, 0), ("ao", "E", 1, 0), ("ax", "F", 1, 3), ("by", 0, 2),
    ("bo", 0, 3), ("fq", 3), ("ax", "E", 1, 3), ("un", 0, 0), ("ac", 0, 1), ("ao", "F", 1, 1), ("ao", "F", 1, 2),
    ("by", 1, 3), ("ao", "E", 1, 1), ("ao", "E", 1, 2), ("ao", "E", 1, 3), ("ao", "F", 1, 3), ("bo", 0, 1),
    ("bs", 1, 2), ("ax", "E", 0, 3), ("ac", 1, 1), ("ax", "F", 0, 0), ("mu", 0, 0, 0), ("bo", 1, 1),
    ("ax", "F", 0, 2), ("ax", "E", 0, 2), ("un", 1, 1), ("ax", "E", 0, 1), ("bo", 1, 0), ("ax", "F", 0, 3),
    ("bo", 0, 2), ("ac", 3, 1), ("ax", "F", 0, 1), ("un", 0, 1), ("bo", 1, 3), ("un", 3, 1), ("mu", 1, 0, 0),
    ("ao", "E", 0, 0), ("ac", 2, 1), ("mu", 1, 3, 0), ("un", 2, 1), ("mu", 1, 1, 0), ("by", 1, 2), ("mu", 1, 2, 0),
    ("cs", 0), ("ao", "F", 0, 0), ("mu", 1, 0, 1), ("mu", 1, 3, 1), ("bo", 1, 2), ("ao", "E", 0, 2), ("mu", 1, 1, 1),
    ("mu", 1, 2, 1), ("ao", "F", 0, 2), ("cs", 1), ("ac", 3, 0), ("mu", 0, 0, 1), ("ao", "F", 0, 1), ("ac", 1, 0),
    ("ao", "E", 0, 1), ("ao", "E", 0, 3), ("ao", "F", 0, 3), ("cr", 0), ("un", 3, 0), ("un", 1, 0), ("mu", 0, 3, 0),
    ("mu", 0, 1, 1), ("mu", 0, 3, 1), ("ac", 2, 0), ("mu", 0, 1, 0), ("cr", 1), ("un", 2, 0), ("mu", 0, 2, 0),
    ("mu", 0, 2, 1),
]


def perform(op, env):
    kind = op[0]
    if kind == "bs":
        h, d = op[1:]
        env.send("EF", ("b", h, -d % 4, 0), dict(dx=d), lambda: env.spread(h, d))
    elif kind == "by":
        h, dl = op[1:]
        if dl:
            env.need("EF", ("b", h, dl, 0))
        for d in (1, -1):
            env.send("EF", ("b", h, dl, -d % 4), dict(dy=d), lambda: env.across(h, dl))
    elif kind == "bo":
        h, dl = op[1:]
        env.need("EF", ("b", h, dl, 3))
        env.send("EF", ("b", h, dl, 2, 0), dict(dy=1), lambda: env.onward(h, dl, -1, 0))
        env.need("EF", ("b", h, dl, 1))
        env.send("EF", ("b", h, dl, 2, 1), dict(dy=-1), lambda: env.onward(h, dl, 1, 1))
    elif kind == "az":
        for q in range(CUTS):
            env.send("E", ("a", 0, OWN, 0, q), dict(dzl=1), lambda q=q: env.start(OWN, q))
        for q in range(CUTS):
            env.send("F", ("a", 0, OTHER, 0, q), dict(dzh=1, dzl=1), lambda q=q: env.start(OTHER, q))
    elif kind == "fq":
        q = op[1]
        env.need("F", ("a", 0, OTHER, 0, q))
        env.send("F", ("a", 0, OTHER, 0, q), dict(dzl=1), lambda: env.block(0, OTHER, q, 0))
    elif kind == "ax":
        types, s, q = op[1:]
        env.need(types, ("a", 0, s, 0, q))
        for d in (1, -1):
            env.send(types, ("a", -d % 4, s, 0, q), dict(dx=d), lambda d=d: env.block(0, s, q, -d % 4))
    elif kind == "ao":
        types, s, q = op[1:]
        dx, d = (3, 1) if q < CUTS // 2 else (1, -1)
        env.need(types, ("a", dx, s, 0, q))
        env.send(types, ("a", 2, s, 0, q), dict(dx=d), lambda: env.block(dx, s, q, 2))
    elif kind == "av":
        types, s, q = op[1:]
        env.need(types, ("a", 2, s, 0, q))
        env.send(types, ("a", 2, s, 0, q), dict(dzl=1), lambda: env.block(2, s, q, 2))
    elif kind == "ac":
        dx, s = op[1:]
        for q in range(CUTS):
            env.need("EF", ("a", dx, s, 0, q))
        env.send("EF", ("a", dx, s, 1), dict(dc=1), lambda: env.twin(dx, s))
    elif kind == "un":
        dx, s = op[1:]
        for q in range(CUTS):
            env.need("EF", ("a", dx, s, 0, q))
        env.need("EF", ("a", dx, s, 1))
        env.compute("unpack", dx, s)
    elif kind == "mu":
        s, dl, h = op[1:]
        env.need("EF", ("b", h, dl, 0))
        env.need("EF", ("b", h, dl, 1), ("b", h, dl, 3), ("b", h, dl, 2, 0), ("b", h, dl, 2, 1))
        env.compute("multiply", s, dl, h)
    elif kind == "cs":
        h = op[1]
        env.compute("code", h)
        env.send("EF", ("s", h), dict(dzh=1), lambda: env.steps(h))
        for q in range(PARTS):
            env.send("EF", ("c", h, q), dict(dzh=1), lambda q=q: env.part(h, q))
    elif kind == "cr":
        h = op[1]
        env.need("EF", ("s", h))
        for q in range(PARTS):
            env.need("EF", ("c", h, q))
            env.compute("add", h, q)


def product_kernel(a_occ, b_occ, a_hbm, b_hbm, out, *scratch):
    a_buf = dict(zip(A_KEYS, scratch[:16]))
    m_buf = dict(zip(A_KEYS, scratch[16:32]))
    (a_in, a_cut, b_in, packed, slots, after, kept, b_buf, dense, partial, coded, coded_in, steps, steps_in, send_sem, recv_sem, local_sem) = scratch[32:]
    row, col, x = lax.axis_index("row"), lax.axis_index("col"), lax.axis_index("layer")
    zh, y, zl, c = row // 4, lax.rem(row, 4), col // 2, lax.rem(col, 2)
    even = zh == zl
    odd = jnp.logical_not(even)

    def at_layer(dx):
        return lax.rem(x + dx + 4, 4)

    def device(dx=0, dy=0, dzh=0, dzl=0, dc=0):
        return (
            lax.rem(zh + dzh, 2) * 4 + lax.rem(y + dy + 4, 4),
            lax.rem(zl + dzl, 2) * 2 + lax.rem(c + dc, 2),
            at_layer(dx),
        )

    get_b = pltpu.make_async_copy(b_hbm.at[0], b_in, local_sem.at[0])
    get_a = pltpu.make_async_copy(a_hbm, a_in, local_sem.at[1])
    get_b.start()
    get_a.start()
    neighbours = [
        dict(dx=1), dict(dx=-1), dict(dx=2), dict(dy=1), dict(dy=-1), dict(dzl=1), dict(dzh=1), dict(dzh=1, dzl=1), dict(dc=1)
    ]
    barrier = pltpu.get_barrier_semaphore()
    for n in neighbours:
        pl.semaphore_signal(barrier, inc=1, device_id=device(**n), device_id_type=MESH)

    numbers, places, used = {}, {}, [0]
    beside = device(dx=1)
    started = {"EF": [], "E": [], "F": []}
    waited = {"E": set(), "F": set()}
    begun = set()

    def when(types, fn):
        if types == "EF":
            fn()
        else:
            pl.when(even if types == "E" else odd)(fn)

    def remote(src, dst, n, m, to):
        return pltpu.make_async_remote_copy(
            src_ref=src, dst_ref=dst, send_sem=send_sem.at[m], recv_sem=recv_sem.at[n], device_id=to, device_id_type=MESH
        )

    def put(types, key, src, dst, to):
        n = numbers.setdefault(key, len(numbers))
        m = used[0]
        used[0] += 1
        remote(src, dst, n, m, device(**to)).start()
        places[key] = dst
        started[types].append((src, dst, n, m))

    def take(key):
        if key[0] == "own":
            own_copy().wait()
            return
        dst = places[key]
        remote(dst, dst, numbers[key], 0, beside).wait_recv()

    def piece(h, dl, dy, part=None):
        start = lax.rem(y + dy + 4, 4) * PIECE
        size = PIECE
        if part is not None:
            size = PIECE // 2
            start = start + part * size
        return b_buf.at[h, at_layer(dl), pl.ds(pl.multiple_of(start, size), size)]

    def tiles(ref, q):
        return ref.at[pl.ds(q * CUT, CUT)]

    def own_copy():
        return pltpu.make_async_copy(packed, a_buf[0, OWN, 0].at[pl.ds(0, CAPS)], local_sem.at[4])

    class Env:
        def need(self, types, *keys):
            late = {"EF": [], "E": [], "F": []}
            for key in keys:
                full = [key]
                if key[0] == "a" and (key[3] == 1 or key[4] == 0):
                    full = [("m",) + key[1:4], key]
                for name in full:
                    todo = {}
                    for t in types:
                        k = ("own",) if t == "E" and name[0] in "am" and name[1:4] == (0, OWN, 0) else name
                        if k[0] == "b" and k[2:] == (0, 0):
                            k = ("mine", k[1])
                        if k not in waited[t]:
                            waited[t].add(k)
                            todo[t] = k
                    if len(todo) == 2 and todo["E"] == todo["F"]:
                        late["EF"].append(todo["E"])
                    else:
                        for t, k in todo.items():
                            late[t].append(k)
            for t, ks in late.items():
                if ks:

                    def waits(ks=ks):
                        for k in ks:
                            if k[0] == "mine":
                                mine(k[1]).wait()
                            else:
                                take(k)

                    when(t, waits)

        def send(self, types, key, to, refs):
            def go():
                for name, src, dst in refs():
                    put(types, name or key, src, dst, to)

            when(types, go)

        def compute(self, what, *args):
            dict(unpack=unpack, multiply=multiply, code=code, add=add)[what](*args)

        def spread(self, h, d):
            return [(None, kept.at[at_layer(d), h], b_buf.at[h, x, pl.ds(pl.multiple_of(y * PIECE, PIECE), PIECE)])]

        def across(self, h, dl):
            return [(None, kept.at[x, h] if dl == 0 else piece(h, dl, 0), piece(h, dl, 0))]

        def onward(self, h, dl, dy, part):
            return [(None, piece(h, dl, dy, part), piece(h, dl, dy, part))]

        def start(self, s, q):
            slow = [(("m", 0, s, 0), slots, m_buf[0, s, 0])] if q == 0 else []
            return slow + [(None, tiles(packed, q), tiles(a_buf[0, s, 0], q))]

        def block(self, dx, s, q, to):
            slow = [(("m", to, s, 0), m_buf[dx, s, 0], m_buf[to, s, 0])] if q == 0 else []
            return slow + [(None, tiles(a_buf[dx, s, 0], q), tiles(a_buf[to, s, 0], q))]

        def twin(self, dx, s):
            here, there = pl.ds(0, CAPS), (dx, s, 1)
            return [
                (("m", dx, s, 1), m_buf[dx, s, 0], m_buf[there]),
                (None, a_buf[dx, s, 0].at[here], a_buf[there].at[here]),
            ]

        def steps(self, h):
            return [(None, steps.at[h], steps_in.at[h])]

        def part(self, h, q):
            rows = pl.ds(q * PART, PART)
            return [(None, coded.at[h, rows], coded_in.at[h, rows])]

    def mine(h):
        return pltpu.make_async_copy(kept.at[x, h], piece(h, 0, 0), local_sem.at[2 + h])

    def unpack(dx, s):
        for dc in range(2):
            key = (dx, s, dc)
            group = lax.rem(c + dc, 2)

            def tile_row(i, carry, key=key, group=group):
                at = pl.ds(pl.multiple_of(i * TILE, TILE), TILE)
                for j in range(GROUPT):
                    slot = m_buf[key][i * GROUPT + j]
                    dense[s, dx, group, at, j * TILE : (j + 1) * TILE] = a_buf[key][slot]
                return carry

            lax.fori_loop(0, ROWT, tile_row, 0)

    def multiply(s, dl, h):
        into = partial.at[h] if s == OTHER else out.at[:, pl.ds(h * SIDE, SIDE)]
        term = jnp.dot(dense[s, dl, 0], b_buf[h, at_layer(dl), :GROUP], preferred_element_type=jnp.float32)
        term += jnp.dot(dense[s, dl, 1], b_buf[h, at_layer(dl), GROUP:], preferred_element_type=jnp.float32)
        if (s, h) in begun:
            into[...] += term
        else:
            into[...] = term
        begun.add((s, h))

    def code(h):
        for q in range(PARTS):
            part = pl.ds(q * PART, PART)
            block = partial[h, part]
            most = jnp.max(jnp.abs(block), axis=0, keepdims=True)
            some = most > SMALLEST
            steps[h, q : q + 1] = jnp.where(some, most * (1.0 / LEVELS), 0.0)
            ups = jnp.where(some, LEVELS / jnp.where(some, most, 1.0), 0.0)
            coded[h, part] = jnp.round(block * ups).astype(jnp.int32).astype(jnp.int16)

    def add(h, q):
        part = pl.ds(q * PART, PART)
        out[part, pl.ds(h * SIDE, SIDE)] += coded_in[h, part].astype(jnp.float32) * steps_in[h, q : q + 1]

    def pack():
        def scan(i, nxt):
            t = SLOTS - 1 - i
            here = a_occ[t // GROUPT, lax.rem(t, GROUPT)] != 0
            nxt = jnp.where(here, t, nxt)
            after[t] = nxt
            return nxt

        after[SLOTS] = SLOTS - 1
        first = lax.fori_loop(0, SLOTS, scan, jnp.int32(SLOTS - 1))

        def name(t, used):
            here = a_occ[t // GROUPT, lax.rem(t, GROUPT)] != 0
            slots[t] = jnp.where(here, used, CAPS)
            return used + jnp.where(here, 1, 0)

        lax.fori_loop(0, SLOTS, name, jnp.int32(0))

        def place(s, t):
            packed[s] = a_cut[t]
            return after[t + 1]

        for t in range(SLOTS):
            i, j = divmod(t, GROUPT)
            a_cut[t] = a_in[i * TILE : (i + 1) * TILE, j * TILE : (j + 1) * TILE]

        lax.fori_loop(0, CAPS, place, first)

    for key in A_KEYS:
        a_buf[key][CAPS] = jnp.zeros((TILE, TILE), jnp.bfloat16)

    env = Env()
    get_a.wait()
    pack()
    pl.semaphore_wait(barrier, len(neighbours))
    perform(("az",), env)

    @pl.when(even)
    def _():
        own_copy().start()

        def keep_slot(t, carry):
            m_buf[0, OWN, 0][t] = slots[t]
            return carry

        lax.fori_loop(0, SLOTS, keep_slot, 0)

    get_b.wait()
    for part in range(NX):
        for i in range(BROWT):
            for k in range(COLT // NX):
                j = part * (COLT // NX) + k
                h, at = divmod(k, COLT // NX // SIDES)
                tile = b_in[i * TILE : (i + 1) * TILE, j * TILE : (j + 1) * TILE]
                present = b_occ[0, i, j] != 0
                kept[part, h, i * TILE : (i + 1) * TILE, at * TILE : (at + 1) * TILE] = jnp.where(
                    present, tile, jnp.zeros_like(tile)
                )
    for h in range(SIDES):
        mine(h).start()

    for op in PLAN:
        perform(op, env)

    for types, copies in started.items():

        def sent(copies=copies):
            for src, dst, n, m in copies:
                remote(src, dst, n, m, beside).wait_send()

        when(types, sent)


def shards(a_tiles, a_occ, b_tiles, b_occ):
    anywhere = pl.BlockSpec(memory_space=pl.ANY)
    smem = pl.BlockSpec(memory_space=pltpu.SMEM)
    return pl.pallas_call(
        product_kernel,
        out_shape=jax.ShapeDtypeStruct((ROWS, NCOLS), jnp.float32),
        in_specs=[smem, smem, anywhere, anywhere],
        out_specs=pl.BlockSpec(memory_space=pltpu.VMEM),
        scratch_shapes=[pltpu.VMEM((CAPS + 1, TILE, TILE), jnp.bfloat16)] * 16
        + [pltpu.SMEM((128,), jnp.int32)] * 16
        + [
            pltpu.VMEM((ROWS, GROUP), jnp.bfloat16),
            pltpu.VMEM((SLOTS, TILE, TILE), jnp.bfloat16),
            pltpu.VMEM((PIECE, NX * NCOLS), jnp.bfloat16),
            pltpu.VMEM((CAPS, TILE, TILE), jnp.bfloat16),
            pltpu.SMEM((128,), jnp.int32),
            pltpu.SMEM((128,), jnp.int32),
            pltpu.VMEM((NX, SIDES, PIECE, SIDE), jnp.bfloat16),
            pltpu.VMEM((SIDES, NX, NY * PIECE, SIDE), jnp.bfloat16),
            pltpu.VMEM((2, NX, 2, ROWS, GROUP), jnp.bfloat16),
            pltpu.VMEM((SIDES, ROWS, SIDE), jnp.float32),
            pltpu.VMEM((SIDES, ROWS, SIDE), jnp.int16),
            pltpu.VMEM((SIDES, ROWS, SIDE), jnp.int16),
            pltpu.VMEM((SIDES, 8, SIDE), jnp.float32),
            pltpu.VMEM((SIDES, 8, SIDE), jnp.float32),
            pltpu.SemaphoreType.DMA((200,)),
            pltpu.SemaphoreType.DMA((200,)),
            pltpu.SemaphoreType.DMA((5,)),
        ],
        compiler_params=pltpu.CompilerParams(
            collective_id=0, has_side_effects=True, vmem_limit_bytes=60 * MIB
        ),
        name="product",
    )(a_occ, b_occ, a_tiles, b_tiles)


def solution(mesh):
    placed = (
        P("row", ("col", "layer")),
        P("row", ("col", "layer")),
        P("layer", "row", "col"),
        P("layer", "row", "col"),
    )
    return jax.shard_map(
        shards, mesh=mesh, in_specs=placed, out_specs=P("row", ("col", "layer")), check_vma=False
    )
```

time: 454 us -> 101 us (0.22)
  the two profiles are of different devices: /device:TPU:0 before, /device:TPU:35 now
where the time goes in v2:
time: 101 us; the launch traced here: 100 us
  Pallas kernels  96 us (95%)
  local copies, waits for them, and re-layouts  4.34 us (4%)
    pallas_call x1, Pallas kernels, shards(): pl.pallas_call(product_kernel, out_shape=jax.ShapeDtypeStruct((ROWS, NCOL...  96 us
    unnamed x2, local copies, waits for them, and re-layouts  4.34 us

profile of v2, /device:TPU:35, one launch (start us, length us, event | category | flops | bytes accessed | tf_op | source)
XLA Modules:
  0.0 100.4 jit_solution(2039616662641136047)
XLA Ops:
  0.0 1.3 %copy.5.b_occ = s32[1,3,16]{2,1,0:T(4,128)} copy(s32[1,3,16]{2,0,1:T(1,128)} %param.7) | data formatting | bytes 384 | tf_op args[3]
  1.3 96.0 %product.1 = f32[1024,512]{1,0:T(8,128)} custom-call(s32[8,6]{1,0:T(8,128)} %a_occ.1, s32[1,3,16]{2,1,0:T(4,128)} %copy.5.b_occ, bf16[1024,768]{1,0:T(8,128)(2,1)} %a_hbm.1, bf16[1,384,2048]{2,1,0:T(8,128)(2,1)} %b_hbm.1), custom_call_target="tpu_custom_call" | custom-call | tf_op jit(solution)/shard_map/product/pallas_call | solution.py:390
  97.3 3.1 %copy.7 = f32[1024,512]{1,0:T(8,128)} copy(f32[1024,512]{1,0:T(8,128)} %product.1) | data formatting | bytes 4194304

commit v3 on v2

--- a/solution.py
+++ b/solution.py
@@ -32,21 +32,21 @@
 
 A_KEYS = [(dx, s, dc) for dx in range(4) for s in (OWN, OTHER) for dc in range(2)]
 PLAN = [
-    ("bs", 1, 1), ("bs", 1, 3), ("by", 1, 0), ("bs", 0, 1), ("bs", 0, 3), ("by", 0, 0), ("ax", "E", 0, 0),
-    ("ax", "F", 1, 0), ("fq", 0), ("by", 1, 1), ("fq", 1), ("by", 0, 3), ("bs", 0, 2), ("by", 0, 1),
-    ("ao", "F", 1, 0), ("ax", "E", 1, 0), ("fq", 2), ("ax", "E", 1, 2), ("ax", "E", 1, 1), ("bo", 0, 0),
-    ("ax", "F", 1, 1), ("ax", "F", 1, 2), ("ac", 0, 0), ("ao", "E", 1, 0), ("ax", "F", 1, 3), ("by", 0, 2),
-    ("bo", 0, 3), ("fq", 3), ("ax", "E", 1, 3), ("un", 0, 0), ("ac", 0, 1), ("ao", "F", 1, 1), ("ao", "F", 1, 2),
-    ("by", 1, 3), ("ao", "E", 1, 1), ("ao", "E", 1, 2), ("ao", "E", 1, 3), ("ao", "F", 1, 3), ("bo", 0, 1),
-    ("bs", 1, 2), ("ax", "E", 0, 3), ("ac", 1, 1), ("ax", "F", 0, 0), ("mu", 0, 0, 0), ("bo", 1, 1),
-    ("ax", "F", 0, 2), ("ax", "E", 0, 2), ("un", 1, 1), ("ax", "E", 0, 1), ("bo", 1, 0), ("ax", "F", 0, 3),
-    ("bo", 0, 2), ("ac", 3, 1), ("ax", "F", 0, 1), ("un", 0, 1), ("bo", 1, 3), ("un", 3, 1), ("mu", 1, 0, 0),
-    ("ao", "E", 0, 0), ("ac", 2, 1), ("mu", 1, 3, 0), ("un", 2, 1), ("mu", 1, 1, 0), ("by", 1, 2), ("mu", 1, 2, 0),
-    ("cs", 0), ("ao", "F", 0, 0), ("mu", 1, 0, 1), ("mu", 1, 3, 1), ("bo", 1, 2), ("ao", "E", 0, 2), ("mu", 1, 1, 1),
-    ("mu", 1, 2, 1), ("ao", "F", 0, 2), ("cs", 1), ("ac", 3, 0), ("mu", 0, 0, 1), ("ao", "F", 0, 1), ("ac", 1, 0),
-    ("ao", "E", 0, 1), ("ao", "E", 0, 3), ("ao", "F", 0, 3), ("cr", 0), ("un", 3, 0), ("un", 1, 0), ("mu", 0, 3, 0),
-    ("mu", 0, 1, 1), ("mu", 0, 3, 1), ("ac", 2, 0), ("mu", 0, 1, 0), ("cr", 1), ("un", 2, 0), ("mu", 0, 2, 0),
-    ("mu", 0, 2, 1),
+    ("bs", 1, 2), ("by", 0, 0), ("by", 1, 0), ("bs", 0, 1), ("bs", 0, 3), ("bs", 0, 2), ("by", 1, 2), ("fq", 1),
+    ("bs", 1, 3), ("by", 0, 3), ("ax", "E", 0, 1), ("ax", "F", 1, 1), ("ax", "E", 1, 1), ("ax", "F", 1, 2),
+    ("fq", 0), ("bo", 1, 0), ("ac", 0, 0), ("fq", 3), ("ax", "E", 1, 0), ("by", 0, 2), ("bo", 0, 0), ("fq", 2),
+    ("un", 0, 0), ("ax", "F", 1, 3), ("by", 1, 1), ("ax", "E", 1, 3), ("ax", "E", 1, 2), ("ac", 0, 1),
+    ("ax", "F", 1, 0), ("by", 0, 1), ("bo", 0, 3), ("mu", 0, 0, 1), ("mu", 0, 0, 0), ("ao", "F", 1, 1), ("bs", 1, 1),
+    ("un", 0, 1), ("ao", "E", 1, 3), ("ao", "F", 1, 0), ("ao", "E", 1, 0), ("ac", 3, 1), ("ao", "F", 1, 2),
+    ("ax", "E", 0, 3), ("bo", 0, 2), ("un", 3, 1), ("ao", "F", 1, 3), ("av", "F", 1, 1), ("bo", 0, 1), ("bo", 1, 1),
+    ("ax", "F", 0, 2), ("ac", 1, 1), ("ax", "F", 0, 0), ("ax", "E", 0, 2), ("mu", 1, 0, 0), ("un", 1, 1),
+    ("av", "F", 1, 2), ("ax", "E", 0, 0), ("ax", "F", 0, 1), ("by", 1, 3), ("mu", 1, 1, 0), ("bo", 1, 2),
+    ("ao", "E", 0, 1), ("ac", 2, 1), ("mu", 1, 3, 0), ("un", 2, 1), ("mu", 1, 2, 0), ("cs", 0), ("bo", 1, 3),
+    ("mu", 1, 1, 1), ("ax", "F", 0, 3), ("mu", 1, 2, 1), ("ao", "F", 0, 2), ("ao", "E", 0, 3), ("ao", "F", 0, 1),
+    ("mu", 1, 0, 1), ("mu", 1, 3, 1), ("ac", 1, 0), ("ao", "F", 0, 3), ("ac", 3, 0), ("ao", "F", 0, 0),
+    ("ao", "E", 0, 0), ("ao", "E", 0, 2), ("cs", 1), ("un", 1, 0), ("un", 3, 0), ("mu", 0, 1, 1), ("mu", 0, 3, 0),
+    ("mu", 0, 3, 1), ("cr", 0), ("ac", 2, 0), ("mu", 0, 1, 0), ("un", 2, 0), ("mu", 0, 2, 1), ("mu", 0, 2, 0),
+    ("cr", 1),
 ]
 
 
@@ -117,13 +117,12 @@
         env.need("EF", ("s", h))
         for q in range(PARTS):
             env.need("EF", ("c", h, q))
-            env.compute("add", h, q)
-
-
-def product_kernel(a_occ, b_occ, a_hbm, b_hbm, out, *scratch):
+
+
+def product_kernel(a_occ, b_occ, a_hbm, b_hbm, out, coded_in, steps_in, *scratch):
     a_buf = dict(zip(A_KEYS, scratch[:16]))
     m_buf = dict(zip(A_KEYS, scratch[16:32]))
-    (a_in, a_cut, b_in, packed, slots, after, kept, b_buf, dense, partial, coded, coded_in, steps, steps_in, send_sem, recv_sem, local_sem) = scratch[32:]
+    (a_in, a_cut, b_in, packed, slots, after, kept, b_buf, dense, partial, coded, steps, send_sem, recv_sem, local_sem) = scratch[32:]
     row, col, x = lax.axis_index("row"), lax.axis_index("col"), lax.axis_index("layer")
     zh, y, zl, c = row // 4, lax.rem(row, 4), col // 2, lax.rem(col, 2)
     even = zh == zl
@@ -179,8 +178,14 @@
         if key[0] == "own":
             own_copy().wait()
             return
-        dst = places[key]
-        remote(dst, dst, numbers[key], 0, beside).wait_recv()
+        n = numbers.setdefault(key, len(numbers))
+        if key[0] == "a":
+            dst = tiles(a_buf[key[1:4]], key[4]) if len(key) == 5 else a_buf[key[1:4]].at[pl.ds(0, CAPS)]
+        elif key[0] == "m":
+            dst = m_buf[key[1:4]]
+        else:
+            dst = places[key]
+        remote(dst, dst, n, 0, beside).wait_recv()
 
     def piece(h, dl, dy, part=None):
         start = lax.rem(y + dy + 4, 4) * PIECE
@@ -237,7 +242,7 @@
             when(types, go)
 
         def compute(self, what, *args):
-            dict(unpack=unpack, multiply=multiply, code=code, add=add)[what](*args)
+            dict(unpack=unpack, multiply=multiply, code=code)[what](*args)
 
         def spread(self, h, d):
             return [(None, kept.at[at_layer(d), h], b_buf.at[h, x, pl.ds(pl.multiple_of(y * PIECE, PIECE), PIECE)])]
@@ -264,11 +269,11 @@
             ]
 
         def steps(self, h):
-            return [(None, steps.at[h], steps_in.at[h])]
+            return [(None, steps.at[h], steps_in.at[:, pl.ds(h * SIDE, SIDE)])]
 
         def part(self, h, q):
             rows = pl.ds(q * PART, PART)
-            return [(None, coded.at[h, rows], coded_in.at[h, rows])]
+            return [(None, coded.at[h, rows], coded_in.at[rows, pl.ds(h * SIDE, SIDE)])]
 
     def mine(h):
         return pltpu.make_async_copy(kept.at[x, h], piece(h, 0, 0), local_sem.at[2 + h])
@@ -307,10 +312,6 @@
             ups = jnp.where(some, LEVELS / jnp.where(some, most, 1.0), 0.0)
             coded[h, part] = jnp.round(block * ups).astype(jnp.int32).astype(jnp.int16)
 
-    def add(h, q):
-        part = pl.ds(q * PART, PART)
-        out[part, pl.ds(h * SIDE, SIDE)] += coded_in[h, part].astype(jnp.float32) * steps_in[h, q : q + 1]
-
     def pack():
         def scan(i, nxt):
             t = SLOTS - 1 - i
@@ -365,7 +366,7 @@
                 j = part * (COLT // NX) + k
                 h, at = divmod(k, COLT // NX // SIDES)
                 tile = b_in[i * TILE : (i + 1) * TILE, j * TILE : (j + 1) * TILE]
-                present = b_occ[0, i, j] != 0
+                present = b_occ[i, 0, j] != 0
                 kept[part, h, i * TILE : (i + 1) * TILE, at * TILE : (at + 1) * TILE] = jnp.where(
                     present, tile, jnp.zeros_like(tile)
                 )
@@ -387,11 +388,15 @@
 def shards(a_tiles, a_occ, b_tiles, b_occ):
     anywhere = pl.BlockSpec(memory_space=pl.ANY)
     smem = pl.BlockSpec(memory_space=pltpu.SMEM)
-    return pl.pallas_call(
+    own, coded, steps = pl.pallas_call(
         product_kernel,
-        out_shape=jax.ShapeDtypeStruct((ROWS, NCOLS), jnp.float32),
+        out_shape=(
+            jax.ShapeDtypeStruct((ROWS, NCOLS), jnp.float32),
+            jax.ShapeDtypeStruct((ROWS, NCOLS), jnp.int16),
+            jax.ShapeDtypeStruct((PARTS, NCOLS), jnp.float32),
+        ),
         in_specs=[smem, smem, anywhere, anywhere],
-        out_specs=pl.BlockSpec(memory_space=pltpu.VMEM),
+        out_specs=(pl.BlockSpec(memory_space=pltpu.VMEM), anywhere, anywhere),
         scratch_shapes=[pltpu.VMEM((CAPS + 1, TILE, TILE), jnp.bfloat16)] * 16
         + [pltpu.SMEM((128,), jnp.int32)] * 16
         + [
@@ -406,9 +411,7 @@
             pltpu.VMEM((2, NX, 2, ROWS, GROUP), jnp.bfloat16),
             pltpu.VMEM((SIDES, ROWS, SIDE), jnp.float32),
             pltpu.VMEM((SIDES, ROWS, SIDE), jnp.int16),
-            pltpu.VMEM((SIDES, ROWS, SIDE), jnp.int16),
-            pltpu.VMEM((SIDES, 8, SIDE), jnp.float32),
-            pltpu.VMEM((SIDES, 8, SIDE), jnp.float32),
+            pltpu.VMEM((SIDES, PARTS, SIDE), jnp.float32),
             pltpu.SemaphoreType.DMA((200,)),
             pltpu.SemaphoreType.DMA((200,)),
             pltpu.SemaphoreType.DMA((5,)),
@@ -417,7 +420,10 @@
             collective_id=0, has_side_effects=True, vmem_limit_bytes=60 * MIB
         ),
         name="product",
-    )(a_occ, b_occ, a_tiles, b_tiles)
+    )(a_occ, b_occ.transpose(1, 0, 2), a_tiles, b_tiles)
+    cut = (PARTS, PART, NCOLS)
+    other = coded.reshape(cut).astype(jnp.float32) * steps[:, None, :]
+    return (own.reshape(cut) + other).reshape(ROWS, NCOLS)
 
 
 def solution(mesh):

time: 101 us -> 94.1 us (0.932)
  the two profiles are of different devices: /device:TPU:35 before, /device:TPU:0 now
where the time goes in v3:
time: 94.1 us; the launch traced here: 94 us
  Pallas kernels  90.3 us (96%)
  other arithmetic  3.66 us (4%)
    pallas_call x1, Pallas kernels, shards(): pl.pallas_call(product_kernel, out_shape=(jax.ShapeDtypeStruct((ROWS, NCO...  90.3 us
    add x1, other arithmetic, shards(): return (own.reshape(cut) + other).reshape(ROWS, NCOLS)  3.66 us

profile of v3, /device:TPU:0, one launch (start us, length us, event | category | flops | bytes accessed | tf_op | source)
XLA Modules:
  0.0 94.0 jit_solution(5192184838503428156)
XLA Ops:
  0.0 90.3 %product.1 = (f32[1024,512]{1,0:T(8,128)}, s16[1024,512]{1,0:T(8,128)(2,1)}, f32[4,512]{1,0:T(4,128)}) custom-call(s32[8,6]{1,0:T(8,128)} %a_occ.1, s32[3,1,16]{2,1,0:T(1,128)} %bitcast.5, bf16[1024,768]{1,0:T(8,128)(2,1)} %a_hbm.1, bf16[1,384,2048]{2,1,0:T(8,128)(2,1)} %b_hbm.1), custom_call_target="tpu_custom_call" | custom-call | tf_op jit(solution)/shard_map/product/pallas_call | solution.py:391
  90.3 3.7 %fusion = f32[1024,512]{1,0:T(8,128)} fusion(f32[1024,512]{1,0:T(8,128)} %get-tuple-element.8, s16[1024,512]{1,0:T(8,128)(2,1)} %get-tuple-element.9, f32[4,512]{1,0:T(4,128)} %get-tuple-element.10), kind=kLoop, calls=%fused_computation.1 | loop fusion | flops 1572864 | bytes 5251072 | tf_op jit(solution)/shard_map/add | solution.py:426

commit v4 on v3

--- a/solution.py
+++ b/solution.py
@@ -287,19 +287,21 @@
                 at = pl.ds(pl.multiple_of(i * TILE, TILE), TILE)
                 for j in range(GROUPT):
                     slot = m_buf[key][i * GROUPT + j]
-                    dense[s, dx, group, at, j * TILE : (j + 1) * TILE] = a_buf[key][slot]
+                    across = pl.ds(pl.multiple_of(group * GROUP + j * TILE, TILE), TILE)
+                    dense[s, dx, at, across] = a_buf[key][slot]
                 return carry
 
-            lax.fori_loop(0, ROWT, tile_row, 0)
+            lax.fori_loop(0, ROWT, tile_row, 0, unroll=True)
 
     def multiply(s, dl, h):
         into = partial.at[h] if s == OTHER else out.at[:, pl.ds(h * SIDE, SIDE)]
-        term = jnp.dot(dense[s, dl, 0], b_buf[h, at_layer(dl), :GROUP], preferred_element_type=jnp.float32)
-        term += jnp.dot(dense[s, dl, 1], b_buf[h, at_layer(dl), GROUP:], preferred_element_type=jnp.float32)
-        if (s, h) in begun:
-            into[...] += term
-        else:
-            into[...] = term
+        for m in range(4):
+            at = pl.ds(m * (ROWS // 4), ROWS // 4)
+            term = jnp.dot(dense[s, dl, at], b_buf[h, at_layer(dl)], preferred_element_type=jnp.float32)
+            if (s, h) in begun:
+                into[at] += term
+            else:
+                into[at] = term
         begun.add((s, h))
 
     def code(h):
@@ -408,7 +410,7 @@
             pltpu.SMEM((128,), jnp.int32),
             pltpu.VMEM((NX, SIDES, PIECE, SIDE), jnp.bfloat16),
             pltpu.VMEM((SIDES, NX, NY * PIECE, SIDE), jnp.bfloat16),
-            pltpu.VMEM((2, NX, 2, ROWS, GROUP), jnp.bfloat16),
+            pltpu.VMEM((2, NX, ROWS, 2 * GROUP), jnp.bfloat16),
             pltpu.VMEM((SIDES, ROWS, SIDE), jnp.float32),
             pltpu.VMEM((SIDES, ROWS, SIDE), jnp.int16),
             pltpu.VMEM((SIDES, PARTS, SIDE), jnp.float32),

time: 94.1 us -> 92.5 us (0.983)
  Pallas kernels: 90.3 us -> 88.1 us
    pallas_call x1, Pallas kernels: 90.3 us -> 88.1 us  [shards(): pl.pallas_call(product_kernel, out_shape=(jax.ShapeDtypeStruct((ROWS, NCO...]
where the time goes in v4:
time: 92.5 us; the launch traced here: 91.8 us
  Pallas kernels  88.1 us (95%)
  other arithmetic  3.66 us (4%)
    pallas_call x1, Pallas kernels, shards(): pl.pallas_call(product_kernel, out_shape=(jax.ShapeDtypeStruct((ROWS, NCO...  88.1 us
    add x1, other arithmetic, shards(): return (own.reshape(cut) + other).reshape(ROWS, NCOLS)  3.66 us

profile of v4, /device:TPU:0, one launch (start us, length us, event | category | flops | bytes accessed | tf_op | source)
XLA Modules:
  0.0 91.8 jit_solution(851586630743718456)
XLA Ops:
  0.0 88.1 %product.1 = (f32[1024,512]{1,0:T(8,128)}, s16[1024,512]{1,0:T(8,128)(2,1)}, f32[4,512]{1,0:T(4,128)}) custom-call(s32[8,6]{1,0:T(8,128)} %a_occ.1, s32[3,1,16]{2,1,0:T(1,128)} %bitcast.5, bf16[1024,768]{1,0:T(8,128)(2,1)} %a_hbm.1, bf16[1,384,2048]{2,1,0:T(8,128)(2,1)} %b_hbm.1), custom_call_target="tpu_custom_call" | custom-call | tf_op jit(solution)/shard_map/product/pallas_call | solution.py:393
  88.1 3.7 %fusion = f32[1024,512]{1,0:T(8,128)} fusion(f32[1024,512]{1,0:T(8,128)} %get-tuple-element.8, s16[1024,512]{1,0:T(8,128)(2,1)} %get-tuple-element.9, f32[4,512]{1,0:T(4,128)} %get-tuple-element.10), kind=kLoop, calls=%fused_computation.1 | loop fusion | flops 1572864 | bytes 5251072 | tf_op jit(solution)/shard_map/add | solution.py:428

commit v5 on v4

--- a/solution.py
+++ b/solution.py
@@ -387,6 +387,11 @@
         when(types, sent)
 
 
+def add_kernel(own, coded, steps, out):
+    i = pl.program_id(0)
+    out[...] = own[...] + coded[...].astype(jnp.float32) * steps[pl.ds(i, 1)]
+
+
 def shards(a_tiles, a_occ, b_tiles, b_occ):
     anywhere = pl.BlockSpec(memory_space=pl.ANY)
     smem = pl.BlockSpec(memory_space=pltpu.SMEM)
@@ -423,9 +428,16 @@
         ),
         name="product",
     )(a_occ, b_occ.transpose(1, 0, 2), a_tiles, b_tiles)
-    cut = (PARTS, PART, NCOLS)
-    other = coded.reshape(cut).astype(jnp.float32) * steps[:, None, :]
-    return (own.reshape(cut) + other).reshape(ROWS, NCOLS)
+    by_part = pl.BlockSpec((PART, NCOLS), lambda i: (i, 0))
+    return pl.pallas_call(
+        add_kernel,
+        grid=(PARTS,),
+        out_shape=jax.ShapeDtypeStruct((ROWS, NCOLS), jnp.float32),
+        in_specs=[by_part, by_part, pl.BlockSpec((PARTS, NCOLS), lambda i: (0, 0))],
+        out_specs=by_part,
+        compiler_params=pltpu.CompilerParams(vmem_limit_bytes=60 * MIB),
+        name="add",
+    )(own, coded, steps)
 
 
 def solution(mesh):

time: 92.5 us -> 92.9 us (level)
  Pallas kernels: 88.1 us -> 92.1 us
  other arithmetic: 3.66 us -> 0 us
    pallas_call x0 -> x1, Pallas kernels: none -> 4.02 us  [shards(): pl.pallas_call(add_kernel, grid=(PARTS,), out_shape=jax.ShapeDtypeStruct(...]
    add x1 -> x0, other arithmetic: 3.66 us -> none  [shards(): return (own.reshape(cut) + other).reshape(ROWS, NCOLS)]
where the time goes in v5:
time: 92.9 us; the launch traced here: 92.2 us
  Pallas kernels  92.1 us (99%)
    pallas_call x1, Pallas kernels, shards(): pl.pallas_call(product_kernel, out_shape=(jax.ShapeDtypeStruct((ROWS, NCO...  88.1 us
    pallas_call x1, Pallas kernels, shards(): pl.pallas_call(add_kernel, grid=(PARTS,), out_shape=jax.ShapeDtypeStruct(...  4.02 us

profile of v5, /device:TPU:0, one launch (start us, length us, event | category | flops | bytes accessed | tf_op | source)
XLA Modules:
  0.0 92.2 jit_solution(6342036552111069298)
XLA Ops:
  0.0 88.1 %product.1 = (f32[1024,512]{1,0:T(8,128)}, s16[1024,512]{1,0:T(8,128)(2,1)}, f32[4,512]{1,0:T(4,128)}) custom-call(s32[8,6]{1,0:T(8,128)} %a_occ.1, s32[3,1,16]{2,1,0:T(1,128)} %bitcast.1, bf16[1024,768]{1,0:T(8,128)(2,1)} %a_hbm.1, bf16[1,384,2048]{2,1,0:T(8,128)(2,1)} %b_hbm.1), custom_call_target="tpu_custom_call" | custom-call | tf_op jit(solution)/shard_map/product/pallas_call | solution.py:398
  88.1 4.0 %add.1 = f32[1024,512]{1,0:T(8,128)} custom-call(f32[1024,512]{1,0:T(8,128)} %get-tuple-element.8.own, s16[1024,512]{1,0:T(8,128)(2,1)} %get-tuple-element.9.coded, f32[4,512]{1,0:T(4,128)} %get-tuple-element.10.steps), custom_call_target="tpu_custom_call" | custom-call | tf_op jit(solution)/shard_map/add/pallas_call | solution.py:432

commit v6 on v4

--- a/solution.py
+++ b/solution.py
@@ -32,20 +32,20 @@
 
 A_KEYS = [(dx, s, dc) for dx in range(4) for s in (OWN, OTHER) for dc in range(2)]
 PLAN = [
-    ("bs", 1, 2), ("by", 0, 0), ("by", 1, 0), ("bs", 0, 1), ("bs", 0, 3), ("bs", 0, 2), ("by", 1, 2), ("fq", 1),
-    ("bs", 1, 3), ("by", 0, 3), ("ax", "E", 0, 1), ("ax", "F", 1, 1), ("ax", "E", 1, 1), ("ax", "F", 1, 2),
-    ("fq", 0), ("bo", 1, 0), ("ac", 0, 0), ("fq", 3), ("ax", "E", 1, 0), ("by", 0, 2), ("bo", 0, 0), ("fq", 2),
-    ("un", 0, 0), ("ax", "F", 1, 3), ("by", 1, 1), ("ax", "E", 1, 3), ("ax", "E", 1, 2), ("ac", 0, 1),
-    ("ax", "F", 1, 0), ("by", 0, 1), ("bo", 0, 3), ("mu", 0, 0, 1), ("mu", 0, 0, 0), ("ao", "F", 1, 1), ("bs", 1, 1),
-    ("un", 0, 1), ("ao", "E", 1, 3), ("ao", "F", 1, 0), ("ao", "E", 1, 0), ("ac", 3, 1), ("ao", "F", 1, 2),
-    ("ax", "E", 0, 3), ("bo", 0, 2), ("un", 3, 1), ("ao", "F", 1, 3), ("av", "F", 1, 1), ("bo", 0, 1), ("bo", 1, 1),
-    ("ax", "F", 0, 2), ("ac", 1, 1), ("ax", "F", 0, 0), ("ax", "E", 0, 2), ("mu", 1, 0, 0), ("un", 1, 1),
-    ("av", "F", 1, 2), ("ax", "E", 0, 0), ("ax", "F", 0, 1), ("by", 1, 3), ("mu", 1, 1, 0), ("bo", 1, 2),
-    ("ao", "E", 0, 1), ("ac", 2, 1), ("mu", 1, 3, 0), ("un", 2, 1), ("mu", 1, 2, 0), ("cs", 0), ("bo", 1, 3),
-    ("mu", 1, 1, 1), ("ax", "F", 0, 3), ("mu", 1, 2, 1), ("ao", "F", 0, 2), ("ao", "E", 0, 3), ("ao", "F", 0, 1),
-    ("mu", 1, 0, 1), ("mu", 1, 3, 1), ("ac", 1, 0), ("ao", "F", 0, 3), ("ac", 3, 0), ("ao", "F", 0, 0),
-    ("ao", "E", 0, 0), ("ao", "E", 0, 2), ("cs", 1), ("un", 1, 0), ("un", 3, 0), ("mu", 0, 1, 1), ("mu", 0, 3, 0),
-    ("mu", 0, 3, 1), ("cr", 0), ("ac", 2, 0), ("mu", 0, 1, 0), ("un", 2, 0), ("mu", 0, 2, 1), ("mu", 0, 2, 0),
+    ("bs", 0, 2), ("bs", 1, 3), ("bs", 0, 1), ("by", 0, 0), ("bs", 1, 1), ("bs", 0, 3), ("by", 1, 0), ("fq", 0),
+    ("by", 0, 2), ("ax", "F", 1, 0), ("fq", 1), ("fq", 2), ("ax", "E", 1, 0), ("bs", 1, 2), ("bo", 0, 0),
+    ("by", 0, 3), ("by", 0, 1), ("ao", "F", 1, 0), ("ax", "E", 1, 1), ("ax", "E", 1, 2), ("by", 1, 3), ("bo", 1, 0),
+    ("ax", "F", 1, 3), ("ax", "E", 1, 3), ("fq", 3), ("bo", 0, 3), ("ax", "F", 1, 2), ("ac", 0, 0), ("ac", 0, 1),
+    ("un", 0, 1), ("ao", "F", 1, 3), ("un", 0, 0), ("bo", 0, 2), ("bo", 0, 1), ("av", "F", 1, 0), ("bo", 1, 3),
+    ("ao", "F", 1, 2), ("ao", "E", 1, 1), ("ao", "E", 1, 2), ("ax", "E", 0, 2), ("ax", "F", 1, 1), ("ax", "F", 0, 0),
+    ("ax", "E", 0, 0), ("av", "F", 1, 3), ("mu", 1, 0, 1), ("by", 1, 2), ("mu", 1, 0, 0), ("ac", 3, 1),
+    ("ao", "F", 1, 1), ("by", 1, 1), ("un", 3, 1), ("ax", "F", 0, 1), ("ax", "E", 0, 1), ("ac", 1, 1),
+    ("ax", "F", 0, 3), ("mu", 1, 3, 0), ("ax", "E", 0, 3), ("un", 1, 1), ("mu", 1, 1, 0), ("ac", 2, 1),
+    ("mu", 0, 0, 1), ("ax", "F", 0, 2), ("un", 2, 1), ("bo", 1, 2), ("mu", 1, 2, 0), ("cs", 0), ("ao", "F", 0, 0),
+    ("ao", "E", 0, 2), ("mu", 0, 0, 0), ("bo", 1, 1), ("mu", 1, 2, 1), ("ao", "F", 0, 3), ("ao", "F", 0, 1),
+    ("ao", "E", 0, 0), ("ao", "E", 0, 1), ("mu", 1, 3, 1), ("mu", 1, 1, 1), ("ac", 3, 0), ("ao", "F", 0, 2),
+    ("cs", 1), ("ao", "E", 0, 3), ("ac", 1, 0), ("un", 3, 0), ("un", 1, 0), ("cr", 0), ("mu", 0, 3, 0),
+    ("mu", 0, 3, 1), ("mu", 0, 1, 1), ("ac", 2, 0), ("mu", 0, 1, 0), ("un", 2, 0), ("mu", 0, 2, 0), ("mu", 0, 2, 1),
     ("cr", 1),
 ]
 

time: 92.5 us -> 95.6 us (1.034)
  Pallas kernels: 88.1 us -> 90.5 us
    pallas_call x1, Pallas kernels: 88.1 us -> 90.5 us  [shards(): pl.pallas_call(product_kernel, out_shape=(jax.ShapeDtypeStruct((ROWS, NCO...]
where the time goes in v6:
time: 95.6 us; the launch traced here: 94.2 us
  Pallas kernels  90.5 us (95%)
  other arithmetic  3.66 us (4%)
    pallas_call x1, Pallas kernels, shards(): pl.pallas_call(product_kernel, out_shape=(jax.ShapeDtypeStruct((ROWS, NCO...  90.5 us
    add x1, other arithmetic, shards(): return (own.reshape(cut) + other).reshape(ROWS, NCOLS)  3.66 us

profile of v6, /device:TPU:0, one launch (start us, length us, event | category | flops | bytes accessed | tf_op | source)
XLA Modules:
  0.0 94.2 jit_solution(9920192384074773198)
XLA Ops:
  0.0 90.5 %product.1 = (f32[1024,512]{1,0:T(8,128)}, s16[1024,512]{1,0:T(8,128)(2,1)}, f32[4,512]{1,0:T(4,128)}) custom-call(s32[8,6]{1,0:T(8,128)} %a_occ.1, s32[3,1,16]{2,1,0:T(1,128)} %bitcast.5, bf16[1024,768]{1,0:T(8,128)(2,1)} %a_hbm.1, bf16[1,384,2048]{2,1,0:T(8,128)(2,1)} %b_hbm.1), custom_call_target="tpu_custom_call" | custom-call | tf_op jit(solution)/shard_map/product/pallas_call | solution.py:393
  90.6 3.7 %fusion = f32[1024,512]{1,0:T(8,128)} fusion(f32[1024,512]{1,0:T(8,128)} %get-tuple-element.8, s16[1024,512]{1,0:T(8,128)(2,1)} %get-tuple-element.9, f32[4,512]{1,0:T(4,128)} %get-tuple-element.10), kind=kLoop, calls=%fused_computation.1 | loop fusion | flops 1572864 | bytes 5251072 | tf_op jit(solution)/shard_map/add | solution.py:428

commit v7 on v4

--- a/solution.py
+++ b/solution.py
@@ -348,19 +348,6 @@
     env = Env()
     get_a.wait()
     pack()
-    pl.semaphore_wait(barrier, len(neighbours))
-    perform(("az",), env)
-
-    @pl.when(even)
-    def _():
-        own_copy().start()
-
-        def keep_slot(t, carry):
-            m_buf[0, OWN, 0][t] = slots[t]
-            return carry
-
-        lax.fori_loop(0, SLOTS, keep_slot, 0)
-
     get_b.wait()
     for part in range(NX):
         for i in range(BROWT):
@@ -374,6 +361,19 @@
                 )
     for h in range(SIDES):
         mine(h).start()
+    pl.semaphore_wait(barrier, len(neighbours))
+    perform(("az",), env)
+
+    @pl.when(even)
+    def _():
+        own_copy().start()
+
+        def keep_slot(t, carry):
+            m_buf[0, OWN, 0][t] = slots[t]
+            return carry
+
+        lax.fori_loop(0, SLOTS, keep_slot, 0)
+
 
     for op in PLAN:
         perform(op, env)

time: 92.5 us -> 92.9 us (level)
  no operation moved by 1% of the time
where the time goes in v7:
time: 92.9 us; the launch traced here: 92 us
  Pallas kernels  88.3 us (95%)
  other arithmetic  3.66 us (4%)
    pallas_call x1, Pallas kernels, shards(): pl.pallas_call(product_kernel, out_shape=(jax.ShapeDtypeStruct((ROWS, NCO...  88.3 us
    add x1, other arithmetic, shards(): return (own.reshape(cut) + other).reshape(ROWS, NCOLS)  3.66 us

profile of v7, /device:TPU:0, one launch (start us, length us, event | category | flops | bytes accessed | tf_op | source)
XLA Modules:
  0.0 92.0 jit_solution(10741871985855979268)
XLA Ops:
  0.0 88.3 %product.1 = (f32[1024,512]{1,0:T(8,128)}, s16[1024,512]{1,0:T(8,128)(2,1)}, f32[4,512]{1,0:T(4,128)}) custom-call(s32[8,6]{1,0:T(8,128)} %a_occ.1, s32[3,1,16]{2,1,0:T(1,128)} %bitcast.5, bf16[1024,768]{1,0:T(8,128)(2,1)} %a_hbm.1, bf16[1,384,2048]{2,1,0:T(8,128)(2,1)} %b_hbm.1), custom_call_target="tpu_custom_call" | custom-call | tf_op jit(solution)/shard_map/product/pallas_call | solution.py:393
  88.4 3.7 %fusion = f32[1024,512]{1,0:T(8,128)} fusion(f32[1024,512]{1,0:T(8,128)} %get-tuple-element.8, s16[1024,512]{1,0:T(8,128)(2,1)} %get-tuple-element.9, f32[4,512]{1,0:T(4,128)} %get-tuple-element.10), kind=kLoop, calls=%fused_computation.1 | loop fusion | flops 1572864 | bytes 5251072 | tf_op jit(solution)/shard_map/add | solution.py:428
